TPU v7x, 32 devices: a whole 2x2x4 slice. The times are simulated.
32 devices in a mesh: grp: 2 (over x), quad: 2 (over core), box: 8 (over z, y).
Axes of the slice: x: 2, y: 2, z: 4, core: 2. Of those that a mesh axis runs over, the one named last changes fastest.
Arguments:
- charges: float32 [4, 256, 64, 512], P(('grp', 'quad'), 'box'), parts along dimension 0, may hold values from -6 to 6
- src_factors: bfloat16 [4, 2, 64, 256, 256], P(('grp', 'quad'), None, 'box'), parts along dimension 0, may hold values from -0.375 to 0.375
- tgt_factors: bfloat16 [4, 1, 64, 256, 256], P(('grp', 'quad'), None, 'box'), parts along dimension 0, may hold values from -0.375 to 0.375
- leaf_factors: bfloat16 [128, 256, 256], P(('grp', 'box')), parts along dimension 0, may hold values from -0.375 to 0.375
- src_connect: int32 [2, 2, 256], P('quad', None, 'box'), may hold values from 0 to 255, as said below
- tgt_connect: int32 [2, 256], P(None, 'box'), may hold values from 0 to 255, as said below
Outputs:
- potentials: float32 [512, 64, 512], P(('grp', 'box'), None, 'quad'), parts along dimension 0
There are 2 independent parts, one for each index of `grp`. A program takes and returns all parts, laid end to end along the dimension named above; an argument that names none is the same for every part. Nothing has to cross between parts.
Inputs may be any that keep to these rules, and one draw needn't show every extreme that they name: `src_connect`: each aligned block of 32 entries of a row is a permutation of that block's own positions in the row. `tgt_connect`: each aligned block of 32 entries of a row is a permutation of that block's own positions in the row.
All inputs are finite; a program needn't handle non-finite values.
Results may differ from a plain program's by a relative error of at most 0.0003.
Values may be sent and summed in bfloat16 or wider, within the bound.
A program may use at most 64 MiB of HBM per device.

v0:
```python
import jax
import jax.numpy as jnp
from jax import lax
from jax.sharding import PartitionSpec as P


def apply_level(current, connect, factors):
    node_count, rank_size, col_count = current.shape
    local_rows = connect % node_count
    gathered = jnp.take(current, local_rows, axis=0).reshape(
        node_count // 4, 4 * rank_size, col_count
    )
    result = jnp.einsum(
        "gij,gjc->gic", factors.astype(jnp.float32), gathered, precision=lax.Precision.HIGHEST
    )
    return result.reshape(node_count, rank_size, col_count)


def per_device(charges, src_factors, tgt_factors, leaf_factors, src_connect, tgt_connect):
    current = charges[0]
    for level_index in range(src_connect.shape[1]):
        current = apply_level(current, src_connect[0, level_index], src_factors[0, level_index])
    target_levels = tgt_connect.shape[0]
    columns = lax.all_to_all(current, "box", split_axis=0, concat_axis=0, tiled=True)
    level_index = 0
    columns = apply_level(columns, tgt_connect[level_index], tgt_factors[0][level_index])
    summed = lax.psum_scatter(columns, "quad", scatter_dimension=2, tiled=True)
    return apply_level(summed, tgt_connect[target_levels - 1], leaf_factors)


def solution(mesh):
    placed = (
        P(("grp", "quad"), "box", None, None),
        P(("grp", "quad"), None, "box", None, None),
        P(("grp", "quad"), None, "box", None, None),
        P(("grp", "box"), None, None),
        P("quad", None, "box"),
        P(None, "box"),
    )
    return jax.shard_map(
        per_device,
        mesh=mesh,
        in_specs=placed,
        out_specs=P(("grp", "box"), None, "quad"),
        check_vma=False,
    )
```

profile of v0, /device:TPU:1, one launch (start us, length us, event | category | flops | bytes accessed | tf_op | source)
XLA Modules:
  0.0 168.3 jit_solution(11645618582597477168)
XLA Ops:
  6.5 0.0 copy-start
  6.5 0.8 compare_and_fusion.2
  7.4 4.9 %gather_fusion.1 = f32[32,64,512]{2,1,0:T(8,128)} fusion(f32[32,64,512]{2,1,0:T(8,128)} %bitcast.53, s32[1024]{0:T(1024)S(1)} %get-tuple-element.15), kind=kCustom, calls=%fused_computation.clone | custom fusion | bytes 8388736 | tf_op jit(solution)/shard_map/jit(_take)/gather | solution.py:10
  12.3 0.0 copy-start.1
  12.3 2.9 %broadcast_select_fusion.2 = f32[32,64,512]{2,1,0:T(8,128)S(1)} fusion(f32[32,64,512]{2,1,0:T(8,128)} %gather_fusion.1, pred[32]{0:T(512)(128)(4,1)S(1)} %get-tuple-element.12), kind=kLoop, calls=%fused_computation.7 | loop fusion | flops 1048576 | bytes 8388640 | tf_op jit(solution)/shard_map/jit(_take)/select_n | solution.py:10
  15.2 0.0 copy-done.1
  15.2 4.3 %fusion.4 = f32[8,512,256]{1,2,0:T(8,128)} fusion(f32[8,256,512]{2,1,0:T(8,128)S(1)} %bitcast.49, bf16[1,2,8,256,256]{4,3,2,1,0:T(8,128)(2,1)S(1)} %copy-done.1), kind=kOutput, calls=%fused_computation.12 | convolution fusion | flops 3221225472 | bytes 9437184 | tf_op jit(solution)/shard_map/gij,gjc->gic/dot_general | solution.py:13
  19.5 5.0 %gather_fusion.2 = f32[32,64,512]{2,1,0:T(8,128)} fusion(f32[32,64,512]{2,1,0:T(8,128)} %bitcast.48, s32[1024]{0:T(1024)S(1)} %get-tuple-element.14), kind=kCustom, calls=%fused_computation.1.clone | custom fusion | bytes 8388736 | tf_op jit(solution)/shard_map/jit(_take)/gather | solution.py:10
  24.5 2.8 %broadcast_select_fusion.1 = f32[32,64,512]{2,1,0:T(8,128)S(1)} fusion(f32[32,64,512]{2,1,0:T(8,128)} %gather_fusion.2, pred[32]{0:T(512)(128)(4,1)S(1)} %get-tuple-element.8), kind=kLoop, calls=%fused_computation.6 | loop fusion | flops 1048576 | bytes 8388640 | tf_op jit(solution)/shard_map/jit(_take)/select_n | solution.py:10
  27.3 4.3 %fusion.2 = f32[8,512,256]{1,2,0:T(8,128)} fusion(f32[8,256,512]{2,1,0:T(8,128)S(1)} %bitcast.50, bf16[1,2,8,256,256]{4,3,2,1,0:T(8,128)(2,1)S(1)} %copy-done.1), kind=kOutput, calls=%fused_computation.10 | convolution fusion | flops 3221225472 | bytes 9437184 | tf_op jit(solution)/shard_map/gij,gjc->gic/dot_general | solution.py:13
  31.6 0.0 copy-start.3
  31.6 6.5 %all-to-all-start = ((f32[32,64,512]{2,1,0:T(8,128)}), f32[32,64,512]{2,1,0:T(8,128)}, u32[]{:S(2)}, u32[]{:S(2)}) async-start(f32[32,64,512]{2,1,0:T(8,128)} %bitcast.47), calls=%async_computation | async-start | bytes 8388608 | tf_op jit(solution)/shard_map/all_to_all | solution.py:24
  38.1 0.2 reduce-scatter.2.cloned.1.call-start
  38.3 0.0 copy-done.3
  38.3 92.2 %all-to-all-done = f32[32,64,512]{2,1,0:T(8,128)} async-done(((f32[32,64,512]{2,1,0:T(8,128)}), f32[32,64,512]{2,1,0:T(8,128)}, u32[]{:S(2)}, u32[]{:S(2)}) %all-to-all-start) | async-done | bytes 4194336 | tf_op jit(solution)/shard_map/all_to_all | solution.py:24
  130.5 5.0 %gather_fusion.3 = f32[32,64,512]{2,1,0:T(8,128)} fusion(f32[32,64,512]{2,1,0:T(8,128)} %all-to-all-done, s32[1024]{0:T(1024)S(1)} %pad_clamp_fusion.1), kind=kCustom, calls=%fused_computation.2.clone | custom fusion | bytes 8388736 | tf_op jit(solution)/shard_map/jit(_take)/gather | solution.py:10
  135.5 2.8 %broadcast_select_fusion = f32[32,64,512]{2,1,0:T(8,128)S(1)} fusion(f32[32,64,512]{2,1,0:T(8,128)} %gather_fusion.3, pred[32]{0:T(512)(128)(4,1)S(1)} %get-tuple-element.6), kind=kLoop, calls=%fused_computation.5 | loop fusion | flops 1048576 | bytes 8388640 | tf_op jit(solution)/shard_map/jit(_take)/select_n | solution.py:10
  138.2 0.0 copy-done
  138.3 4.3 %fusion = f32[8,512,256]{1,2,0:T(8,128)} fusion(f32[8,256,512]{2,1,0:T(8,128)S(1)} %bitcast.51, bf16[1,1,8,256,256]{4,3,2,1,0:T(8,128)(2,1)S(1)} %copy-done), kind=kOutput, calls=%fused_computation.8 | convolution fusion | flops 3221225472 | bytes 9437184 | tf_op jit(solution)/shard_map/gij,gjc->gic/dot_general | solution.py:13
  142.5 0.0 reduce-scatter.2.cloned.1.call-update
  142.6 0.1 squeeze.23
  142.7 0.1 broadcast_in_dim.23
  142.7 0.1 broadcast_in_dim.24
  142.9 12.6 %reduce-scatter.2.cloned.1.call-done = f32[32,64,256]{2,1,0:T(8,128)} async-done(((f32[32,64,512]{2,1,0:T(8,128)}), f32[32,64,256]{2,1,0:T(8,128)}) %reduce-scatter.2.cloned.1.call-update) | async-done | bytes 2097168 | tf_op jit(solution)/shard_map/reduce_scatter | solution.py:27
  155.4 2.3 %gather_fusion = f32[32,64,256]{2,1,0:T(8,128)S(1)} fusion(f32[32,64,256]{2,1,0:T(8,128)} %reduce-scatter.2.cloned.1.call-done, s32[1024]{0:T(1024)S(1)} %pad_clamp_fusion), kind=kCustom, calls=%fused_computation.3 | custom fusion | bytes 4194432 | tf_op jit(solution)/shard_map/jit(_take)/gather | solution.py:10
  157.7 0.0 copy-start.2
  157.7 0.3 bitcast_select_fusion
  158.1 0.9 copy-done.2
  158.9 2.6 %fusion.14 = f32[8,256,256]{1,2,0:T(8,128)} fusion(f32[8,256,256]{2,1,0:T(8,128)S(1)} %bitcast_select_fusion, bf16[8,256,256]{2,1,0:T(8,128)(2,1)S(1)} %copy-done.2), kind=kOutput, calls=%fused_computation.51 | convolution fusion | flops 1610612736 | bytes 5242880 | tf_op jit(solution)/shard_map/gij,gjc->gic/dot_general | solution.py:13
  (7 shorter events, 0.1 us)
Async XLA Ops:
  6.5 131.7 %copy-start = (bf16[1,1,8,256,256]{4,3,2,1,0:T(8,128)(2,1)S(1)}, bf16[1,1,8,256,256]{4,3,2,1,0:T(8,128)(2,1)}, u32[]{:S(2)}) copy-start(bf16[1,1,8,256,256]{4,3,2,1,0:T(8,128)(2,1)} %param.10) | copy-start | bytes 3145732
  12.3 2.9 %copy-start.1 = (bf16[1,2,8,256,256]{4,3,2,1,0:T(8,128)(2,1)S(1)}, bf16[1,2,8,256,256]{4,3,2,1,0:T(8,128)(2,1)}, u32[]{:S(2)}) copy-start(bf16[1,2,8,256,256]{4,3,2,1,0:T(8,128)(2,1)} %param.9) | copy-start | bytes 6291460
  31.6 6.7 %copy-start.3 = (s32[2,32]{1,0:T(2,128)S(1)}, s32[2,32]{1,0:T(2,128)}, u32[]{:S(2)}) copy-start(s32[2,32]{1,0:T(2,128)} %param.13) | copy-start | bytes 772
  31.6 98.9 %all-to-all-start = ((f32[32,64,512]{2,1,0:T(8,128)}), f32[32,64,512]{2,1,0:T(8,128)}, u32[]{:S(2)}, u32[]{:S(2)}) async-start(f32[32,64,512]{2,1,0:T(8,128)} %bitcast.47), calls=%async_computation | async-start | bytes 8388608 | tf_op jit(solution)/shard_map/all_to_all | solution.py:24
  38.1 117.4 %reduce-scatter.2.cloned.1.call-start = ((), (), s32[]{:S(2)}) async-start(), calls=%async_computation.2 | async-start | bytes 6291456 | tf_op jit(solution)/shard_map/reduce_scatter | solution.py:27
  157.7 1.2 copy-start.2
Sparse Core Ops, SparseCore 0:
  142.7 12.7 reduce-scatter.1
where the time goes:
time: 169 us; the launch traced here: 168 us
  waiting for transfers between devices  105 us (62%)
  local copies, waits for them, and re-layouts  18.3 us (11%)
  matrix products  15.4 us (9%)
  between operations  13.5 us (8%)
  other arithmetic  9.68 us (6%)
  starting transfers between devices  6.73 us (4%)
    all_to_all x1, waiting for transfers between devices, per_device(): lax.all_to_all(current, 'box', split_axis=0, concat_axis=0, tiled=True)  92.2 us
    gather x4, local copies, waits for them, and re-layouts, apply_level(): jnp.take(current, local_rows, axis=0)  17.2 us
    dot_general x4, matrix products, apply_level(): jnp.einsum('gij,gjc->gic', factors.astype(jnp.float32), gathered, precisi...  15.4 us
    reduce_scatter x1, waiting for transfers between devices, per_device(): summed = lax.psum_scatter(columns, 'quad', scatter_dimension=2, tiled=True)  12.6 us
    select_n x5, other arithmetic, apply_level(): jnp.take(current, local_rows, axis=0)  8.83 us
    all_to_all x1, starting transfers between devices, per_device(): lax.all_to_all(current, 'box', split_axis=0, concat_axis=0, tiled=True)  6.51 us
  transfers between devices with their start and end apart: 2, of which 2 were waited for; matrix products, arithmetic and copies ran while one was open for 0% of the time, Pallas kernels for 0%

commit v1 on v0

v1 whole, which is shorter than its diff:
```python
import functools

import jax
import jax.numpy as jnp
from jax import lax
from jax.experimental import pallas as pl
from jax.experimental.pallas import tpu as pltpu
from jax.sharding import PartitionSpec as P

MESH = pl.DeviceIdType.MESH
WIDTH = 128
LARGEST = 32767.0
ROUNDER = 12582912.0
SMALLEST = 1e-33


def partner(me, step, count):
    if count & (count - 1):
        return lax.rem(me + step, count)
    other = 0
    bit = 1
    while bit < count:
        mine = lax.rem(lax.div(me, bit), 2)
        theirs = lax.rem(lax.div(step, bit), 2)
        other = other + bit * (mine + theirs - 2 * mine * theirs)
        bit *= 2
    return other


def product(factor, values):
    high = values.astype(jnp.bfloat16)
    low = (values - high.astype(jnp.float32)).astype(jnp.bfloat16)
    return jnp.dot(factor, high, preferred_element_type=jnp.float32) + jnp.dot(
        factor, low, preferred_element_type=jnp.float32
    )


def kernel(cfg, src_con, tgt_con, charges, src_f, tgt_f, leaf_f, out, *scratch):
    boxes, quads, nodes, rank, per, chunks, levels, share, unit = cfg
    steps = chunks * quads
    groups = nodes // per
    scales = share // unit
    take = iter(scratch)
    held = [next(take) for _ in range(steps)]
    sent = [next(take) for _ in range(steps)]
    sent_scale = [next(take) for _ in range(steps)]
    got = [next(take) for _ in range(chunks)]
    got_scale = [next(take) for _ in range(chunks)]
    done = [next(take) for _ in range(chunks)]
    work, middle, src_v, tgt_v, leaf_v = [next(take) for _ in range(5)]
    (held_sem, src_sem, tgt_sem, leaf_sem, own_sem, out_sem,
     swap_send, swap_recv, send, recv, scale_send, scale_recv) = list(take)

    grp = lax.axis_index("grp")
    quad = lax.axis_index("quad")
    box = lax.axis_index("box")

    def quad_at(ahead):
        return lax.rem(quad + ahead, quads)

    def device(ahead, other):
        return {"grp": grp, "quad": quad_at(ahead), "box": other}

    barrier = pltpu.get_barrier_semaphore()
    for ahead in range(quads):
        for d in range(boxes):
            if ahead or d:
                pl.semaphore_signal(
                    barrier, inc=1, device_id=device(ahead, partner(box, d, boxes)),
                    device_id_type=MESH,
                )

    half = chunks * WIDTH
    loads = []
    for s in range(steps):
        c, ahead = s // quads, s % quads
        column = pl.multiple_of(quad_at(ahead) * half + c * WIDTH, WIDTH)
        loads.append(pltpu.make_async_copy(
            charges.at[0, :, :, pl.ds(column, WIDTH)], held[s], held_sem.at[s]))
    src_loads = [
        pltpu.make_async_copy(src_f.at[0, l], src_v.at[l], src_sem.at[l]) for l in range(levels)
    ]
    tgt_load = pltpu.make_async_copy(tgt_f.at[0, 0], tgt_v.at[0], tgt_sem)
    leaf_load = pltpu.make_async_copy(leaf_f, leaf_v, leaf_sem)
    loads[0].start()
    for load in src_loads + loads[1:] + [tgt_load, leaf_load]:
        load.start()

    def gather(read, connect, g):
        return jnp.concatenate(
            [read(lax.rem(connect(per * g + k), nodes)) for k in range(per)], axis=0
        )

    def source(s):
        for l in range(levels):
            before = held[s] if l == 0 else work.at[(l - 1) % 2]

            def body(g, carry, l=l):
                values = gather(
                    (lambda i: held[s][i]) if l == 0 else (lambda i: work[(l - 1) % 2, i]),
                    lambda slot: src_con[0, l, slot], g,
                )
                result = product(src_v[l, g], values)
                if l < levels - 1:
                    work[l % 2, pl.ds(per * g, per)] = result.reshape(per, rank, WIDTH)
                else:
                    parts = result.reshape(per // unit, unit * rank, WIDTH)
                    top = jnp.maximum(
                        jnp.max(jnp.abs(parts), axis=1, keepdims=True), SMALLEST)
                    sent_scale[s][pl.ds(per // unit * g, per // unit)] = top * (1.0 / LARGEST)
                    whole = (parts * (LARGEST / top) + ROUNDER) - ROUNDER
                    sent[s][pl.ds(per * g, per)] = (
                        whole.astype(jnp.int32).astype(jnp.int16).reshape(per, rank, WIDTH))
                return carry

            lax.fori_loop(0, groups, body, 0, unroll=2)

    def copies(s, d):
        c, ahead = s // quads, s % quads
        other = partner(box, d, boxes)
        at = dict(device_id=device(ahead, other), device_id_type=MESH)
        return (
            pltpu.make_async_remote_copy(
                src_ref=sent[s].at[pl.ds(other * share, share)],
                dst_ref=got[c].at[ahead, pl.ds(box * share, share)],
                send_sem=send.at[c, ahead, d], recv_sem=recv.at[c, ahead, d], **at),
            pltpu.make_async_remote_copy(
                src_ref=sent_scale[s].at[pl.ds(other * scales, scales)],
                dst_ref=got_scale[c].at[ahead, pl.ds(box * scales, scales)],
                send_sem=scale_send.at[c, ahead, d], recv_sem=scale_recv.at[c, ahead, d], **at),
        )

    def own_copies(c):
        s = c * quads
        return (
            pltpu.make_async_copy(
                sent[s].at[pl.ds(box * share, share)],
                got[c].at[0, pl.ds(box * share, share)], own_sem.at[c, 0]),
            pltpu.make_async_copy(
                sent_scale[s].at[pl.ds(box * scales, scales)],
                got_scale[c].at[0, pl.ds(box * scales, scales)], own_sem.at[c, 1]),
        )

    def each(s, act):
        first = 0 if s % quads else 1

        def body(n, carry):
            for copy in copies(s, boxes - 1 - n):
                act(copy)
            return carry

        lax.fori_loop(0, boxes - first, body, 0)

    swaps = [
        pltpu.make_async_remote_copy(
            src_ref=tgt_f.at[0, 0], dst_ref=tgt_v.at[ahead],
            send_sem=swap_send.at[ahead], recv_sem=swap_recv.at[ahead],
            device_id=device(ahead, box), device_id_type=MESH)
        for ahead in range(1, quads)
    ]

    for s in range(steps):
        loads[s].wait()
        if s == 0:
            for load in src_loads:
                load.wait()
        source(s)
        if s == 0:
            pl.semaphore_wait(barrier, boxes * quads - 1)
        each(s, lambda copy: copy.start())
        if s % quads == 0:
            for copy in own_copies(s // quads):
                copy.start()
        if s == 0:
            for swap in swaps:
                swap.start()

    tgt_load.wait()
    leaf_load.wait()
    for swap in swaps:
        swap.wait()
    stores = []
    for c in range(chunks):
        for ahead in range(quads):
            each(c * quads + ahead, lambda copy: copy.wait_recv())
        for copy in own_copies(c):
            copy.wait()

        def target(g, carry, c=c):
            total = None
            for ahead in range(quads):
                def read(i, ahead=ahead):
                    return got[c][ahead, i].astype(jnp.int32).astype(jnp.float32) * (
                        got_scale[c][ahead, lax.div(i, unit)])
                term = product(tgt_v[ahead, g], gather(read, lambda slot: tgt_con[0, slot], g))
                total = term if total is None else total + term
            middle[pl.ds(per * g, per)] = total.reshape(per, rank, WIDTH)
            return carry

        lax.fori_loop(0, groups, target, 0, unroll=2)

        def leaf(g, carry, c=c):
            values = gather(lambda i: middle[i], lambda slot: tgt_con[1, slot], g)
            done[c][pl.ds(per * g, per)] = product(leaf_v[g], values).reshape(per, rank, WIDTH)
            return carry

        lax.fori_loop(0, groups, leaf, 0, unroll=2)
        store = pltpu.make_async_copy(
            done[c], out.at[:, :, pl.ds(c * WIDTH, WIDTH)], out_sem.at[c])
        store.start()
        stores.append(store)

    for s in range(steps):
        each(s, lambda copy: copy.wait_send())
    for store in stores:
        store.wait()


def per_device(mesh, charges, src_factors, tgt_factors, leaf_factors, src_connect, tgt_connect):
    boxes, quads = mesh.shape["box"], mesh.shape["quad"]
    _, nodes, rank, columns = charges.shape
    levels, groups, fact = src_factors.shape[1:4]
    per = fact // rank
    share = nodes // boxes
    unit = min(share, per)
    chunks = columns // quads // WIDTH
    steps = chunks * quads
    slab = (nodes, rank, WIDTH)
    cfg = (boxes, quads, nodes, rank, per, chunks, levels, share, unit)
    dma = pltpu.SemaphoreType.DMA
    scratch = (
        [pltpu.VMEM(slab, jnp.float32)] * steps
        + [pltpu.VMEM(slab, jnp.int16)] * steps
        + [pltpu.VMEM((nodes // unit, 1, WIDTH), jnp.float32)] * steps
        + [pltpu.VMEM((quads,) + slab, jnp.int16)] * chunks
        + [pltpu.VMEM((quads, nodes // unit, 1, WIDTH), jnp.float32)] * chunks
        + [pltpu.VMEM(slab, jnp.float32)] * chunks
        + [
            pltpu.VMEM((2,) + slab, jnp.float32),
            pltpu.VMEM(slab, jnp.float32),
            pltpu.VMEM((levels, groups, fact, fact), jnp.bfloat16),
            pltpu.VMEM((quads, groups, fact, fact), jnp.bfloat16),
            pltpu.VMEM((groups, fact, fact), jnp.bfloat16),
            dma((steps,)), dma((levels,)), dma, dma, dma((chunks, 2)), dma((chunks,)),
            dma((quads,)), dma((quads,)),
        ]
        + [dma((chunks, quads, boxes))] * 4
    )
    smem = pl.BlockSpec(memory_space=pltpu.SMEM)
    anywhere = pl.BlockSpec(memory_space=pl.ANY)
    flops = 2 * (levels + 1) * groups * fact * fact * columns
    return pl.pallas_call(
        functools.partial(kernel, cfg),
        out_shape=jax.ShapeDtypeStruct((nodes, rank, columns // quads), jnp.float32),
        in_specs=[smem, smem, anywhere, anywhere, anywhere, anywhere],
        out_specs=anywhere,
        scratch_shapes=scratch,
        compiler_params=pltpu.CompilerParams(
            collective_id=0, has_side_effects=True, vmem_limit_bytes=48 * 2**20
        ),
        cost_estimate=pl.CostEstimate(flops=flops, bytes_accessed=10 * 2**20, transcendentals=0),
    )(src_connect, tgt_connect, charges, src_factors, tgt_factors, leaf_factors)


def solution(mesh):
    placed = (
        P(("grp", "quad"), "box", None, None),
        P(("grp", "quad"), None, "box", None, None),
        P(("grp", "quad"), None, "box", None, None),
        P(("grp", "box"), None, None),
        P("quad", None, "box"),
        P(None, "box"),
    )
    return jax.shard_map(
        functools.partial(per_device, mesh),
        mesh=mesh,
        in_specs=placed,
        out_specs=P(("grp", "box"), None, "quad"),
        check_vma=False,
    )
```

time: 169 us -> 65.4 us (0.39)
  waiting for transfers between devices: 105 us -> 0 us
  Pallas kernels: 0 us -> 60.1 us
  matrix products: 15.4 us -> 0 us
  between operations: 13.5 us -> 0.01 us
  local copies, waits for them, and re-layouts: 18.3 us -> 5.13 us
  other arithmetic: 9.68 us -> 0 us
  starting transfers between devices: 6.73 us -> 0 us
    all_to_all x1 -> x0, waiting for transfers between devices: 92.2 us -> none  [per_device(): lax.all_to_all(current, 'box', split_axis=0, concat_axis=0, tiled=True)]
    pallas_call x0 -> x1, Pallas kernels: none -> 60.1 us  [per_device(): pl.pallas_call(functools.partial(kernel, cfg), out_shape=jax.ShapeDtypeSt...]
    gather x4 -> x0, local copies, waits for them, and re-layouts: 17.2 us -> none  [apply_level(): jnp.take(current, local_rows, axis=0)]
    dot_general x4 -> x0, matrix products: 15.4 us -> none  [apply_level(): jnp.einsum('gij,gjc->gic', factors.astype(jnp.float32), gathered, precisi...]
    reduce_scatter x1 -> x0, waiting for transfers between devices: 12.6 us -> none  [per_device(): summed = lax.psum_scatter(columns, 'quad', scatter_dimension=2, tiled=True)]
    select_n x5 -> x0, other arithmetic: 8.83 us -> none  [apply_level(): jnp.take(current, local_rows, axis=0)]
    all_to_all x1 -> x0, starting transfers between devices: 6.51 us -> none  [per_device(): lax.all_to_all(current, 'box', split_axis=0, concat_axis=0, tiled=True)]
    unnamed x8 -> x9, local copies, waits for them, and re-layouts: 0.89 us -> 5.13 us
  transfers between devices with their start and end apart: 2 -> 0, of which waited for: 2 -> 0; matrix products, arithmetic and copies ran while one was open for 0% -> 0% of each run, Pallas kernels for 0% -> 0%
where the time goes in v1:
time: 65.4 us; the launch traced here: 65.2 us
  Pallas kernels  60.1 us (92%)
  local copies, waits for them, and re-layouts  5.13 us (8%)
    pallas_call x1, Pallas kernels, per_device(): pl.pallas_call(functools.partial(kernel, cfg), out_shape=jax.ShapeDtypeSt...  60.1 us
    unnamed x9, local copies, waits for them, and re-layouts  5.13 us

profile of v1, /device:TPU:1, one launch (start us, length us, event | category | flops | bytes accessed | tf_op | source)
XLA Modules:
  0.0 65.2 jit_solution(17527535762993929161)
XLA Ops:
  0.0 0.0 copy-start
  0.0 1.2 %copy-done = bf16[1,1,8,256,256]{4,3,2,1,0:T(8,128)(2,1)S(1)} copy-done((bf16[1,1,8,256,256]{4,3,2,1,0:T(8,128)(2,1)S(1)}, bf16[1,1,8,256,256]{4,3,2,1,0:T(8,128)(2,1)}, u32[]{:S(2)}) %copy-start) | copy-done | bytes 1048600
  1.2 0.0 copy-start.1
  1.2 1.2 %copy-done.1 = bf16[8,256,256]{2,1,0:T(8,128)(2,1)S(1)} copy-done((bf16[8,256,256]{2,1,0:T(8,128)(2,1)S(1)}, bf16[8,256,256]{2,1,0:T(8,128)(2,1)}, u32[]{:S(2)}) %copy-start.1) | copy-done | bytes 1048600
  2.5 0.0 copy-start.2
  2.5 0.7 %copy-done.2 = s32[1,2,32]{2,1,0:T(2,128)S(1)} copy-done((s32[1,2,32]{2,1,0:T(2,128)S(1)}, s32[1,2,32]{2,1,0:T(2,128)}, u32[]{:S(2)}) %copy-start.2) | copy-done | bytes 280
  3.1 0.0 copy-start.3
  3.1 0.7 %copy-done.3 = s32[2,32]{1,0:T(2,128)S(1)} copy-done((s32[2,32]{1,0:T(2,128)S(1)}, s32[2,32]{1,0:T(2,128)}, u32[]{:S(2)}) %copy-start.3) | copy-done | bytes 280
  3.8 60.1 %shard_map.64 = f32[32,64,256]{2,1,0:T(8,128)S(1)} custom-call(s32[1,2,32]{2,1,0:T(2,128)S(1)} %copy-done.2, s32[2,32]{1,0:T(2,128)S(1)} %copy-done.3, f32[1,32,64,512]{3,2,1,0:T(8,128)} %charges.1, bf16[1,2,8,256,256]{4,3,2,1,0:T(8,128)(2,1)} %src_f.1, bf16[1,1,8,256,256]{4,3,2,1,0:T(8,128)(2,1)S(1)} %copy-done, bf16[8,256,256]{2,1,0:T(8,128)(2,1)S(1)} %copy-done.1), custom_call_target="tpu_custom_call" | custom-call | flops 1610612736 | bytes 10485760 | tf_op jit(solution)/shard_map/pallas_call | solution.py:252
  63.9 1.3 %copy.8 = f32[32,64,256]{2,1,0:T(8,128)} copy(f32[32,64,256]{2,1,0:T(8,128)S(1)} %shard_map.64) | data formatting | bytes 4194304
Async XLA Ops:
  0.0 1.2 %copy-start = (bf16[1,1,8,256,256]{4,3,2,1,0:T(8,128)(2,1)S(1)}, bf16[1,1,8,256,256]{4,3,2,1,0:T(8,128)(2,1)}, u32[]{:S(2)}) copy-start(bf16[1,1,8,256,256]{4,3,2,1,0:T(8,128)(2,1)} %tgt_f.1) | copy-start | bytes 3145732
  1.2 1.2 %copy-start.1 = (bf16[8,256,256]{2,1,0:T(8,128)(2,1)S(1)}, bf16[8,256,256]{2,1,0:T(8,128)(2,1)}, u32[]{:S(2)}) copy-start(bf16[8,256,256]{2,1,0:T(8,128)(2,1)} %leaf_f.1) | copy-start | bytes 3145732
  2.5 0.7 %copy-start.2 = (s32[1,2,32]{2,1,0:T(2,128)S(1)}, s32[1,2,32]{2,1,0:T(2,128)}, u32[]{:S(2)}) copy-start(s32[1,2,32]{2,1,0:T(2,128)} %src_con.1) | copy-start | bytes 772
  3.1 0.7 %copy-start.3 = (s32[2,32]{1,0:T(2,128)S(1)}, s32[2,32]{1,0:T(2,128)}, u32[]{:S(2)}) copy-start(s32[2,32]{1,0:T(2,128)} %tgt_con.1) | copy-start | bytes 772

commit v2 on v1

--- a/solution.py
+++ b/solution.py
@@ -35,7 +35,7 @@
     )
 
 
-def kernel(cfg, src_con, tgt_con, charges, src_f, tgt_f, leaf_f, out, *scratch):
+def kernel(cfg, src_hbm, tgt_hbm, charges, src_f, tgt_f, leaf_f, out, *scratch):
     boxes, quads, nodes, rank, per, chunks, levels, share, unit = cfg
     steps = chunks * quads
     groups = nodes // per
@@ -47,8 +47,8 @@
     got = [next(take) for _ in range(chunks)]
     got_scale = [next(take) for _ in range(chunks)]
     done = [next(take) for _ in range(chunks)]
-    work, middle, src_v, tgt_v, leaf_v = [next(take) for _ in range(5)]
-    (held_sem, src_sem, tgt_sem, leaf_sem, own_sem, out_sem,
+    work, middle, src_v, tgt_v, leaf_v, src_con, tgt_con = [next(take) for _ in range(7)]
+    (con_sem, held_sem, src_sem, tgt_sem, leaf_sem, own_sem, out_sem,
      swap_send, swap_recv, send, recv, scale_send, scale_recv) = list(take)
 
     grp = lax.axis_index("grp")
@@ -60,15 +60,6 @@
 
     def device(ahead, other):
         return {"grp": grp, "quad": quad_at(ahead), "box": other}
-
-    barrier = pltpu.get_barrier_semaphore()
-    for ahead in range(quads):
-        for d in range(boxes):
-            if ahead or d:
-                pl.semaphore_signal(
-                    barrier, inc=1, device_id=device(ahead, partner(box, d, boxes)),
-                    device_id_type=MESH,
-                )
 
     half = chunks * WIDTH
     loads = []
@@ -82,9 +73,21 @@
     ]
     tgt_load = pltpu.make_async_copy(tgt_f.at[0, 0], tgt_v.at[0], tgt_sem)
     leaf_load = pltpu.make_async_copy(leaf_f, leaf_v, leaf_sem)
-    loads[0].start()
-    for load in src_loads + loads[1:] + [tgt_load, leaf_load]:
+    con_loads = [
+        pltpu.make_async_copy(src_hbm, src_con, con_sem.at[0]),
+        pltpu.make_async_copy(tgt_hbm, tgt_con, con_sem.at[1]),
+    ]
+    for load in con_loads + [loads[0]] + src_loads:
         load.start()
+
+    barrier = pltpu.get_barrier_semaphore()
+    for ahead in range(quads):
+        for d in range(boxes):
+            if ahead or d:
+                pl.semaphore_signal(
+                    barrier, inc=1, device_id=device(ahead, partner(box, d, boxes)),
+                    device_id_type=MESH,
+                )
 
     def gather(read, connect, g):
         return jnp.concatenate(
@@ -93,8 +96,6 @@
 
     def source(s):
         for l in range(levels):
-            before = held[s] if l == 0 else work.at[(l - 1) % 2]
-
             def body(g, carry, l=l):
                 values = gather(
                     (lambda i: held[s][i]) if l == 0 else (lambda i: work[(l - 1) % 2, i]),
@@ -113,7 +114,7 @@
                         whole.astype(jnp.int32).astype(jnp.int16).reshape(per, rank, WIDTH))
                 return carry
 
-            lax.fori_loop(0, groups, body, 0, unroll=2)
+            lax.fori_loop(0, groups, body, 0, unroll=True)
 
     def copies(s, d):
         c, ahead = s // quads, s % quads
@@ -145,7 +146,7 @@
         first = 0 if s % quads else 1
 
         def body(n, carry):
-            for copy in copies(s, boxes - 1 - n):
+            for copy in copies(s, n + first):
                 act(copy)
             return carry
 
@@ -162,8 +163,10 @@
     for s in range(steps):
         loads[s].wait()
         if s == 0:
-            for load in src_loads:
+            for load in con_loads + src_loads:
                 load.wait()
+            for load in loads[1:] + [tgt_load, leaf_load]:
+                load.start()
         source(s)
         if s == 0:
             pl.semaphore_wait(barrier, boxes * quads - 1)
@@ -197,14 +200,14 @@
             middle[pl.ds(per * g, per)] = total.reshape(per, rank, WIDTH)
             return carry
 
-        lax.fori_loop(0, groups, target, 0, unroll=2)
+        lax.fori_loop(0, groups, target, 0, unroll=True)
 
         def leaf(g, carry, c=c):
             values = gather(lambda i: middle[i], lambda slot: tgt_con[1, slot], g)
             done[c][pl.ds(per * g, per)] = product(leaf_v[g], values).reshape(per, rank, WIDTH)
             return carry
 
-        lax.fori_loop(0, groups, leaf, 0, unroll=2)
+        lax.fori_loop(0, groups, leaf, 0, unroll=True)
         store = pltpu.make_async_copy(
             done[c], out.at[:, :, pl.ds(c * WIDTH, WIDTH)], out_sem.at[c])
         store.start()
@@ -241,18 +244,20 @@
             pltpu.VMEM((levels, groups, fact, fact), jnp.bfloat16),
             pltpu.VMEM((quads, groups, fact, fact), jnp.bfloat16),
             pltpu.VMEM((groups, fact, fact), jnp.bfloat16),
-            dma((steps,)), dma((levels,)), dma, dma, dma((chunks, 2)), dma((chunks,)),
+            pltpu.SMEM(src_connect.shape, jnp.int32),
+            pltpu.SMEM(tgt_connect.shape, jnp.int32),
+            dma((2,)), dma((steps,)), dma((levels,)), dma, dma, dma((chunks, 2)), dma((chunks,)),
             dma((quads,)), dma((quads,)),
         ]
         + [dma((chunks, quads, boxes))] * 4
     )
-    smem = pl.BlockSpec(memory_space=pltpu.SMEM)
+    fixed = pl.BlockSpec(memory_space=pltpu.HBM)
     anywhere = pl.BlockSpec(memory_space=pl.ANY)
     flops = 2 * (levels + 1) * groups * fact * fact * columns
     return pl.pallas_call(
         functools.partial(kernel, cfg),
         out_shape=jax.ShapeDtypeStruct((nodes, rank, columns // quads), jnp.float32),
-        in_specs=[smem, smem, anywhere, anywhere, anywhere, anywhere],
+        in_specs=[fixed] * 6,
         out_specs=anywhere,
         scratch_shapes=scratch,
         compiler_params=pltpu.CompilerParams(

time: 65.4 us -> 61.2 us (0.936)
  Pallas kernels: 60.1 us -> 55.7 us
    pallas_call x1, Pallas kernels: 60.1 us -> 55.7 us  [per_device(): pl.pallas_call(functools.partial(kernel, cfg), out_shape=jax.ShapeDtypeSt...]
where the time goes in v2:
time: 61.2 us; the launch traced here: 60.8 us
  Pallas kernels  55.7 us (91%)
  local copies, waits for them, and re-layouts  5.13 us (8%)
    pallas_call x1, Pallas kernels, per_device(): pl.pallas_call(functools.partial(kernel, cfg), out_shape=jax.ShapeDtypeSt...  55.7 us
    unnamed x9, local copies, waits for them, and re-layouts  5.13 us

profile of v2, /device:TPU:1, one launch (start us, length us, event | category | flops | bytes accessed | tf_op | source)
XLA Modules:
  0.0 60.8 jit_solution(5464567338464303870)
XLA Ops:
  0.0 0.0 copy-start
  0.0 1.2 %copy-done = bf16[1,1,8,256,256]{4,3,2,1,0:T(8,128)(2,1)S(1)} copy-done((bf16[1,1,8,256,256]{4,3,2,1,0:T(8,128)(2,1)S(1)}, bf16[1,1,8,256,256]{4,3,2,1,0:T(8,128)(2,1)}, u32[]{:S(2)}) %copy-start) | copy-done | bytes 1048600
  1.2 0.0 copy-start.1
  1.2 1.2 %copy-done.1 = bf16[8,256,256]{2,1,0:T(8,128)(2,1)S(1)} copy-done((bf16[8,256,256]{2,1,0:T(8,128)(2,1)S(1)}, bf16[8,256,256]{2,1,0:T(8,128)(2,1)}, u32[]{:S(2)}) %copy-start.1) | copy-done | bytes 1048600
  2.5 0.0 copy-start.2
  2.5 0.7 %copy-done.2 = s32[1,2,32]{2,1,0:T(2,128)S(1)} copy-done((s32[1,2,32]{2,1,0:T(2,128)S(1)}, s32[1,2,32]{2,1,0:T(2,128)}, u32[]{:S(2)}) %copy-start.2) | copy-done | bytes 280
  3.1 0.0 copy-start.3
  3.1 0.7 %copy-done.3 = s32[2,32]{1,0:T(2,128)S(1)} copy-done((s32[2,32]{1,0:T(2,128)S(1)}, s32[2,32]{1,0:T(2,128)}, u32[]{:S(2)}) %copy-start.3) | copy-done | bytes 280
  3.8 55.7 %shard_map.64 = f32[32,64,256]{2,1,0:T(8,128)S(1)} custom-call(s32[1,2,32]{2,1,0:T(2,128)S(1)} %copy-done.2, s32[2,32]{1,0:T(2,128)S(1)} %copy-done.3, f32[1,32,64,512]{3,2,1,0:T(8,128)} %charges.1, bf16[1,2,8,256,256]{4,3,2,1,0:T(8,128)(2,1)} %src_f.1, bf16[1,1,8,256,256]{4,3,2,1,0:T(8,128)(2,1)S(1)} %copy-done, bf16[8,256,256]{2,1,0:T(8,128)(2,1)S(1)} %copy-done.1), custom_call_target="tpu_custom_call" | custom-call | flops 1610612736 | bytes 10485760 | tf_op jit(solution)/shard_map/pallas_call | solution.py:257
  59.5 1.3 %copy.8 = f32[32,64,256]{2,1,0:T(8,128)} copy(f32[32,64,256]{2,1,0:T(8,128)S(1)} %shard_map.64) | data formatting | bytes 4194304
Async XLA Ops:
  0.0 1.2 %copy-start = (bf16[1,1,8,256,256]{4,3,2,1,0:T(8,128)(2,1)S(1)}, bf16[1,1,8,256,256]{4,3,2,1,0:T(8,128)(2,1)}, u32[]{:S(2)}) copy-start(bf16[1,1,8,256,256]{4,3,2,1,0:T(8,128)(2,1)} %tgt_f.1) | copy-start | bytes 3145732
  1.2 1.2 %copy-start.1 = (bf16[8,256,256]{2,1,0:T(8,128)(2,1)S(1)}, bf16[8,256,256]{2,1,0:T(8,128)(2,1)}, u32[]{:S(2)}) copy-start(bf16[8,256,256]{2,1,0:T(8,128)(2,1)} %leaf_f.1) | copy-start | bytes 3145732
  2.5 0.7 %copy-start.2 = (s32[1,2,32]{2,1,0:T(2,128)S(1)}, s32[1,2,32]{2,1,0:T(2,128)}, u32[]{:S(2)}) copy-start(s32[1,2,32]{2,1,0:T(2,128)} %src_hbm.1) | copy-start | bytes 772
  3.1 0.7 %copy-start.3 = (s32[2,32]{1,0:T(2,128)S(1)}, s32[2,32]{1,0:T(2,128)}, u32[]{:S(2)}) copy-start(s32[2,32]{1,0:T(2,128)} %tgt_hbm.1) | copy-start | bytes 772

commit v3 on v2

--- a/solution.py
+++ b/solution.py
@@ -264,7 +264,10 @@
             collective_id=0, has_side_effects=True, vmem_limit_bytes=48 * 2**20
         ),
         cost_estimate=pl.CostEstimate(flops=flops, bytes_accessed=10 * 2**20, transcendentals=0),
-    )(src_connect, tgt_connect, charges, src_factors, tgt_factors, leaf_factors)
+    )(*(
+        pltpu.with_memory_space_constraint(array, pltpu.HBM)
+        for array in (src_connect, tgt_connect, charges, src_factors, tgt_factors, leaf_factors)
+    ))
 
 
 def solution(mesh):

time: 61.2 us -> 57.2 us (0.935)
  local copies, waits for them, and re-layouts: 5.13 us -> 1.32 us
    unnamed x9 -> x1, local copies, waits for them, and re-layouts: 5.13 us -> 1.32 us
where the time goes in v3:
time: 57.2 us; the launch traced here: 56.9 us
  Pallas kernels  55.5 us (97%)
  local copies, waits for them, and re-layouts  1.32 us (2%)
    pallas_call x1, Pallas kernels, per_device(): pl.pallas_call(functools.partial(kernel, cfg), out_shape=jax.ShapeDtypeSt...  55.5 us
    unnamed x1, local copies, waits for them, and re-layouts  1.32 us

profile of v3, /device:TPU:1, one launch (start us, length us, event | category | flops | bytes accessed | tf_op | source)
XLA Modules:
  0.0 56.9 jit_solution(15211510247956102740)
XLA Ops:
  0.0 55.5 %shard_map.64 = f32[32,64,256]{2,1,0:T(8,128)S(1)} custom-call(s32[1,2,32]{2,1,0:T(2,128)} %src_hbm.1, s32[2,32]{1,0:T(2,128)} %tgt_hbm.1, f32[1,32,64,512]{3,2,1,0:T(8,128)} %charges.1, bf16[1,2,8,256,256]{4,3,2,1,0:T(8,128)(2,1)} %src_f.1, bf16[1,1,8,256,256]{4,3,2,1,0:T(8,128)(2,1)} %tgt_f.1, bf16[8,256,256]{2,1,0:T(8,128)(2,1)} %leaf_f.1), custom_call_target="tpu_custom_call" | custom-call | flops 1610612736 | bytes 10485760 | tf_op jit(solution)/shard_map/pallas_call | solution.py:257
  55.6 1.3 %copy.8 = f32[32,64,256]{2,1,0:T(8,128)} copy(f32[32,64,256]{2,1,0:T(8,128)S(1)} %shard_map.64) | data formatting | bytes 4194304

commit v4 on v3

--- a/solution.py
+++ b/solution.py
@@ -44,8 +44,8 @@
     held = [next(take) for _ in range(steps)]
     sent = [next(take) for _ in range(steps)]
     sent_scale = [next(take) for _ in range(steps)]
-    got = [next(take) for _ in range(chunks)]
-    got_scale = [next(take) for _ in range(chunks)]
+    got = [[next(take) for _ in range(quads)] for _ in range(chunks)]
+    got_scale = [[next(take) for _ in range(quads)] for _ in range(chunks)]
     done = [next(take) for _ in range(chunks)]
     work, middle, src_v, tgt_v, leaf_v, src_con, tgt_con = [next(take) for _ in range(7)]
     (con_sem, held_sem, src_sem, tgt_sem, leaf_sem, own_sem, out_sem,
@@ -123,11 +123,11 @@
         return (
             pltpu.make_async_remote_copy(
                 src_ref=sent[s].at[pl.ds(other * share, share)],
-                dst_ref=got[c].at[ahead, pl.ds(box * share, share)],
+                dst_ref=got[c][ahead].at[pl.ds(box * share, share)],
                 send_sem=send.at[c, ahead, d], recv_sem=recv.at[c, ahead, d], **at),
             pltpu.make_async_remote_copy(
                 src_ref=sent_scale[s].at[pl.ds(other * scales, scales)],
-                dst_ref=got_scale[c].at[ahead, pl.ds(box * scales, scales)],
+                dst_ref=got_scale[c][ahead].at[pl.ds(box * scales, scales)],
                 send_sem=scale_send.at[c, ahead, d], recv_sem=scale_recv.at[c, ahead, d], **at),
         )
 
@@ -136,10 +136,10 @@
         return (
             pltpu.make_async_copy(
                 sent[s].at[pl.ds(box * share, share)],
-                got[c].at[0, pl.ds(box * share, share)], own_sem.at[c, 0]),
+                got[c][0].at[pl.ds(box * share, share)], own_sem.at[c, 0]),
             pltpu.make_async_copy(
                 sent_scale[s].at[pl.ds(box * scales, scales)],
-                got_scale[c].at[0, pl.ds(box * scales, scales)], own_sem.at[c, 1]),
+                got_scale[c][0].at[pl.ds(box * scales, scales)], own_sem.at[c, 1]),
         )
 
     def each(s, act):
@@ -186,21 +186,22 @@
     for c in range(chunks):
         for ahead in range(quads):
             each(c * quads + ahead, lambda copy: copy.wait_recv())
-        for copy in own_copies(c):
-            copy.wait()
-
-        def target(g, carry, c=c):
-            total = None
-            for ahead in range(quads):
-                def read(i, ahead=ahead):
-                    return got[c][ahead, i].astype(jnp.int32).astype(jnp.float32) * (
-                        got_scale[c][ahead, lax.div(i, unit)])
+            if ahead == 0:
+                for copy in own_copies(c):
+                    copy.wait()
+
+            def target(g, carry, c=c, ahead=ahead):
+                def read(i):
+                    return got[c][ahead][i].astype(jnp.int32).astype(jnp.float32) * (
+                        got_scale[c][ahead][lax.div(i, unit)])
+
                 term = product(tgt_v[ahead, g], gather(read, lambda slot: tgt_con[0, slot], g))
-                total = term if total is None else total + term
-            middle[pl.ds(per * g, per)] = total.reshape(per, rank, WIDTH)
-            return carry
-
-        lax.fori_loop(0, groups, target, 0, unroll=True)
+                term = term.reshape(per, rank, WIDTH)
+                at = pl.ds(per * g, per)
+                middle[at] = term if ahead == 0 else middle[at] + term
+                return carry
+
+            lax.fori_loop(0, groups, target, 0, unroll=True)
 
         def leaf(g, carry, c=c):
             values = gather(lambda i: middle[i], lambda slot: tgt_con[1, slot], g)
@@ -235,8 +236,8 @@
         [pltpu.VMEM(slab, jnp.float32)] * steps
         + [pltpu.VMEM(slab, jnp.int16)] * steps
         + [pltpu.VMEM((nodes // unit, 1, WIDTH), jnp.float32)] * steps
-        + [pltpu.VMEM((quads,) + slab, jnp.int16)] * chunks
-        + [pltpu.VMEM((quads, nodes // unit, 1, WIDTH), jnp.float32)] * chunks
+        + [pltpu.VMEM(slab, jnp.int16)] * steps
+        + [pltpu.VMEM((nodes // unit, 1, WIDTH), jnp.float32)] * steps
         + [pltpu.VMEM(slab, jnp.float32)] * chunks
         + [
             pltpu.VMEM((2,) + slab, jnp.float32),

time: 57.2 us -> 56.6 us (0.990)
  no operation moved by 1% of the time
where the time goes in v4:
time: 56.6 us; the launch traced here: 56.3 us
  Pallas kernels  55 us (97%)
  local copies, waits for them, and re-layouts  1.32 us (2%)
    pallas_call x1, Pallas kernels, per_device(): pl.pallas_call(functools.partial(kernel, cfg), out_shape=jax.ShapeDtypeSt...  55 us
    unnamed x1, local copies, waits for them, and re-layouts  1.32 us

profile of v4, /device:TPU:1, one launch (start us, length us, event | category | flops | bytes accessed | tf_op | source)
XLA Modules:
  0.0 56.3 jit_solution(15099810925730756235)
XLA Ops:
  0.0 55.0 %shard_map.64 = f32[32,64,256]{2,1,0:T(8,128)S(1)} custom-call(s32[1,2,32]{2,1,0:T(2,128)} %src_hbm.1, s32[2,32]{1,0:T(2,128)} %tgt_hbm.1, f32[1,32,64,512]{3,2,1,0:T(8,128)} %charges.1, bf16[1,2,8,256,256]{4,3,2,1,0:T(8,128)(2,1)} %src_f.1, bf16[1,1,8,256,256]{4,3,2,1,0:T(8,128)(2,1)} %tgt_f.1, bf16[8,256,256]{2,1,0:T(8,128)(2,1)} %leaf_f.1), custom_call_target="tpu_custom_call" | custom-call | flops 1610612736 | bytes 10485760 | tf_op jit(solution)/shard_map/pallas_call | solution.py:258
  55.0 1.3 %copy.8 = f32[32,64,256]{2,1,0:T(8,128)} copy(f32[32,64,256]{2,1,0:T(8,128)S(1)} %shard_map.64) | data formatting | bytes 4194304
